TPU v7x, 32 devices: a whole 2x2x4 slice. The times are simulated.
32 devices in a mesh: dp: 4 (over y, core), fsdp: 4 (over z), seq: 2 (over x).
Axes of the slice: x: 2, y: 2, z: 4, core: 2. Of those that a mesh axis runs over, the one named last changes fastest.
Arguments:
- queries: bfloat16 [16, 256, 2048], P(('dp', 'fsdp'), 'seq'), may hold values from -30 to 30
- key_rows: bfloat16 [16, 256, 2048], P(('dp', 'fsdp'), 'seq'), may hold values from -12 to 12
- value_rows: bfloat16 [16, 256, 2048], P(('dp', 'fsdp'), 'seq'), may hold values from -6 to 6
- cotangent: bfloat16 [16, 256, 2048], P(('dp', 'fsdp'), 'seq'), may hold values from -6 to 6
- out_weight: bfloat16 [2048, 2048], P('fsdp'), may hold values from -0.125 to 0.125
Outputs:
- query_grad: bfloat16 [16, 256, 2048], P(('dp', 'fsdp'), 'seq')
- key_grad: bfloat16 [16, 256, 2048], P(('dp', 'fsdp'), 'seq')
- value_grad: bfloat16 [16, 256, 2048], P(('dp', 'fsdp'), 'seq')
- weight_grad: float32 [2048, 2048], P('fsdp')
All inputs are finite; a program needn't handle non-finite values.
Results may differ from a plain program's by a relative error of at most 0.014.
Values may be sent and summed in bfloat16 or wider, within the bound.
A program may use at most 128 MiB of HBM per device.

v0:
```python
import jax
import jax.numpy as jnp
from jax import lax
from jax.sharding import PartitionSpec as P

DH = 128


def head_backward(query_head, key_head, value_head, grad_head, block_rows):
    length = key_head.shape[0]
    score_scale = DH ** (-0.5)
    blocks = length // block_rows

    def visit(carry, block):
        key_acc, value_acc = carry
        begin = block * block_rows
        query_block = lax.dynamic_slice_in_dim(query_head, begin, block_rows, 0)
        grad_block = lax.dynamic_slice_in_dim(grad_head, begin, block_rows, 0)
        scores = (
            jnp.einsum("qd,kd->qk", query_block, key_head, preferred_element_type=jnp.float32)
            * score_scale
        )
        highest = jnp.max(scores, axis=1, keepdims=True)
        expanded = jnp.exp(scores - highest)
        weights = expanded / jnp.sum(expanded, axis=1, keepdims=True)
        weights_half = weights.astype(jnp.bfloat16)
        attended = jnp.einsum(
            "qk,kd->qd", weights_half, value_head, preferred_element_type=jnp.float32
        ).astype(jnp.bfloat16)
        grad_weights = jnp.einsum(
            "qd,kd->qk", grad_block, value_head, preferred_element_type=jnp.float32
        )
        row_delta = jnp.sum(weights * grad_weights, axis=1, keepdims=True)
        grad_scores = (weights * (grad_weights - row_delta)).astype(jnp.bfloat16)
        query_grad = (
            jnp.einsum("qk,kd->qd", grad_scores, key_head, preferred_element_type=jnp.float32)
            * score_scale
        ).astype(jnp.bfloat16)
        key_acc = key_acc + jnp.einsum(
            "qk,qd->kd", grad_scores, query_block, preferred_element_type=jnp.float32
        )
        value_acc = value_acc + jnp.einsum(
            "qk,qd->kd", weights_half, grad_block, preferred_element_type=jnp.float32
        )
        return ((key_acc, value_acc), (attended, query_grad))

    empty = jnp.zeros(key_head.shape, jnp.float32)
    finals, stacked = lax.scan(visit, (empty, empty), jnp.arange(blocks))
    attended = stacked[0].reshape(length, DH)
    query_grad = stacked[1].reshape(length, DH)
    key_grad = (finals[0] * score_scale).astype(jnp.bfloat16)
    value_grad = finals[1].astype(jnp.bfloat16)
    return (attended, query_grad, key_grad, value_grad)


def attend_heads(query_heads, key_heads, value_heads, grad_heads):
    length = query_heads.shape[1]
    per_device = query_heads.shape[2] // DH
    block_rows = min(512, length)
    gathered = [[], [], [], []]
    for head_index in range(per_device):
        lower = head_index * DH
        upper = lower + DH
        results = head_backward(
            query_heads[0, :, lower:upper],
            key_heads[0, :, lower:upper],
            value_heads[0, :, lower:upper],
            grad_heads[0, :, lower:upper],
            block_rows,
        )
        for position, result in enumerate(results):
            gathered[position].append(result)
    return tuple((jnp.concatenate(group, axis=1)[None] for group in gathered))


def body(queries, key_rows, value_rows, cotangent, out_weight):
    samples = lax.axis_size("dp") * lax.axis_size("fsdp")
    grad_out = jnp.einsum(
        "btd,rd->btr",
        cotangent,
        lax.all_gather(out_weight, "fsdp", axis=0, tiled=True),
        preferred_element_type=jnp.float32,
    ).astype(jnp.bfloat16)
    query_heads, key_heads, value_heads, grad_heads = (
        lax.all_to_all(queries, "seq", split_axis=2, concat_axis=1, tiled=True),
        lax.all_to_all(key_rows, "seq", split_axis=2, concat_axis=1, tiled=True),
        lax.all_to_all(value_rows, "seq", split_axis=2, concat_axis=1, tiled=True),
        lax.all_to_all(grad_out, "seq", split_axis=2, concat_axis=1, tiled=True),
    )
    head_results = attend_heads(query_heads, key_heads, value_heads, grad_heads)
    attended, query_grad, key_grad, value_grad = (
        lax.all_to_all(head_results[0], "seq", split_axis=1, concat_axis=2, tiled=True),
        lax.all_to_all(head_results[1], "seq", split_axis=1, concat_axis=2, tiled=True),
        lax.all_to_all(head_results[2], "seq", split_axis=1, concat_axis=2, tiled=True),
        lax.all_to_all(head_results[3], "seq", split_axis=1, concat_axis=2, tiled=True),
    )
    shares = lax.psum_scatter(
        jnp.einsum("btr,btd->rd", attended, cotangent, preferred_element_type=jnp.float32),
        ("fsdp", "seq"),
        scatter_dimension=0,
        tiled=True,
    )
    shares = lax.psum(shares.astype(jnp.bfloat16), "dp").astype(jnp.float32)
    total = lax.all_gather(shares.astype(jnp.bfloat16), "seq", axis=0, tiled=True).astype(
        shares.dtype
    )
    return (query_grad, key_grad, value_grad, total / samples)


def solution(mesh):
    return jax.shard_map(
        body,
        mesh=mesh,
        in_specs=(
            P(("dp", "fsdp"), "seq", None),
            P(("dp", "fsdp"), "seq", None),
            P(("dp", "fsdp"), "seq", None),
            P(("dp", "fsdp"), "seq", None),
            P("fsdp", None),
        ),
        out_specs=(
            P(("dp", "fsdp"), "seq", None),
            P(("dp", "fsdp"), "seq", None),
            P(("dp", "fsdp"), "seq", None),
            P("fsdp", None),
        ),
        check_vma=False,
    )
```

profile of v0, /device:TPU:0, one launch (start us, length us, event | category | flops | bytes accessed | tf_op | source)
XLA Modules:
  0.0 528.8 jit_solution(7082781794581919626)
XLA Ops:
  8.8 2.4 copy.55
  11.7 11.6 %reduce.1 = bf16[2048,128]{1,0:T(8,128)(2,1)S(1)} reduce(bf16[2048,1,128]{2,1,0:T(2,128)(2,1)S(1)} %bitcast.293, bf16[]{:T(256)} %broadcast.90), dimensions={1}, to_apply=%bitcast.175.reduce_sub_computation | reduce | bytes 1048578
  24.2 4.2 all-to-all-start
  29.2 11.6 %reduce = bf16[2048,128]{1,0:T(8,128)(2,1)S(1)} reduce(bf16[2048,1,128]{2,1,0:T(2,128)(2,1)S(1)} %bitcast.299, bf16[]{:T(256)} %broadcast.90), dimensions={1}, to_apply=%bitcast.177.reduce_sub_computation | reduce | bytes 1048578
  41.6 3.7 all-to-all-start.1
  46.1 11.6 %reduce.2 = bf16[2048,128]{1,0:T(8,128)(2,1)S(1)} reduce(bf16[2048,1,128]{2,1,0:T(2,128)(2,1)S(1)} %bitcast.300, bf16[]{:T(256)} %broadcast.90), dimensions={1}, to_apply=%bitcast.173.reduce_sub_computation | reduce | bytes 1048578
  58.5 3.5 all-to-all-start.3
  65.2 5.5 %all-to-all-done.3 = bf16[2,2,65536]{2,1,0:T(2,128)(2,1)S(1)} async-done(((bf16[2,2,65536]{2,1,0:T(2,128)(2,1)}), bf16[2,2,65536]{2,1,0:T(2,128)(2,1)S(1)}, u32[]{:S(2)}, u32[]{:S(2)}) %all-to-all-start.3) | async-done | bytes 524320 | tf_op jit(solution)/shard_map/all_to_all | solution.py:87
  83.7 2.5 copy.69
  86.2 4.5 reduce.7
  92.1 11.1 %all_to_all.141 = bf16[2,2,65536]{2,1,0:T(2,128)(2,1)} all-to-all(bf16[2,2,65536]{2,1,0:T(2,128)(2,1)S(1)} %reshape.90), channel_id=1, replica_groups=mesh['dp'=4,'fsdp'=4,'seq'=2] {'seq'}, dimensions={0} | all-to-all | bytes 1048576 | tf_op jit(solution)/shard_map/all_to_all | solution.py:92
  106.9 8.0 %fusion.49 = f32[2048,2048]{1,0:T(8,128)} fusion(bf16[128,2048]{0,1:T(8,128)(2,1)S(1)} %bitcast.301, bf16[1,128,2048]{2,1,0:T(8,128)(2,1)S(1)} %copy-done), kind=kOutput, calls=%fused_computation.91 | convolution fusion | flops 1073741824 | bytes 17825792 | tf_op jit(solution)/shard_map/btr,btd->rd/dot_general | solution.py:98
  115.0 48.1 %all-gather.3.cloned.1.call-done = bf16[2048,2048]{1,0:T(8,128)(2,1)} async-done(((bf16[512,2048]{1,0:T(8,128)(2,1)}), bf16[2048,2048]{1,0:T(8,128)(2,1)}) %all-gather.3.cloned.1.call-update) | async-done | bytes 8388624 | tf_op jit(solution)/shard_map/all_gather | solution.py:81
  163.1 7.1 %fusion = bf16[1,128,2048]{2,1,0:T(8,128)(2,1)} fusion(bf16[2048,2048]{1,0:T(8,128)(2,1)} %all-gather.3.cloned.1.call-done, bf16[1,128,2048]{2,1,0:T(8,128)(2,1)S(1)} %copy-done), kind=kOutput, calls=%fused_computation.2 | convolution fusion | flops 1074003968 | bytes 9437184 | tf_op jit(solution)/shard_map/btd,rd->btr/dot_general | solution.py:78
  170.1 2.3 copy.59
  172.5 12.4 %reduce.3 = bf16[2048,128]{1,0:T(8,128)(2,1)} reduce(bf16[2048,1,128]{2,1,0:T(2,128)(2,1)S(1)} %bitcast.296, bf16[]{:T(256)} %broadcast.90), dimensions={1}, to_apply=%bitcast.171.reduce_sub_computation | reduce | bytes 1048578
  186.0 17.7 %all_to_all.142 = bf16[2,2,65536]{2,1,0:T(2,128)(2,1)} all-to-all(bf16[2,2,65536]{2,1,0:T(2,128)(2,1)S(1)} %reshape.76), channel_id=1, replica_groups=mesh['dp'=4,'fsdp'=4,'seq'=2] {'seq'}, dimensions={0} | all-to-all | bytes 1048576 | tf_op jit(solution)/shard_map/all_to_all | solution.py:88
  209.9 2.5 copy.67
  212.4 4.5 reduce.6
  216.9 2.1 reshape.88
  219.1 3.5 all-to-all-start.6
  231.6 201.0 %reduce-scatter.2.cloned.1.call-done = f32[256,2048]{1,0:T(8,128)} async-done(((f32[2048,2048]{1,0:T(8,128)}), f32[256,2048]{1,0:T(8,128)}) %reduce-scatter.2.cloned.1.call-update) | async-done | bytes 2097168 | tf_op jit(solution)/shard_map/reduce_scatter | solution.py:97
  432.5 2.7 convert_element_type.240
  436.8 34.4 %all-reduce.2.cloned.1.call-done = bf16[256,2048]{1,0:T(8,128)(2,1)} async-done(((bf16[256,2048]{1,0:T(8,128)(2,1)}), bf16[256,2048]{1,0:T(8,128)(2,1)}) %all-reduce.2.cloned.1.call-update) | async-done | bytes 1048592 | tf_op jit(solution)/shard_map/psum | solution.py:103
  474.1 3.7 reduce.4
  479.8 3.5 all-to-all-start.4
  485.0 2.5 copy.65
  487.5 3.7 reduce.5
  492.4 5.0 all-to-all-done.4
  497.3 3.5 all-to-all-start.5
  504.8 9.8 %all-to-all-done.5 = bf16[2,2,65536]{2,1,0:T(2,128)(2,1)S(1)} async-done(((bf16[2,2,65536]{2,1,0:T(2,128)(2,1)}), bf16[2,2,65536]{2,1,0:T(2,128)(2,1)S(1)}, u32[]{:S(2)}, u32[]{:S(2)}) %all-to-all-start.5) | async-done | bytes 524320 | tf_op jit(solution)/shard_map/all_to_all | solution.py:94
  516.8 4.2 convert_multiply_fusion
  (148 shorter events, 57.9 us)
Async XLA Ops:
  8.0 98.9 %copy-start = (bf16[1,128,2048]{2,1,0:T(8,128)(2,1)S(1)}, bf16[1,128,2048]{2,1,0:T(8,128)(2,1)}, u32[]{:S(2)}) copy-start(bf16[1,128,2048]{2,1,0:T(8,128)(2,1)} %param.8) | copy-start | bytes 1572868
  8.0 20.4 %copy-start.6 = (bf16[1,128,2048]{2,1,0:T(8,128)(2,1)S(1)}, bf16[1,128,2048]{2,1,0:T(8,128)(2,1)}, u32[]{:S(2)}) copy-start(bf16[1,128,2048]{2,1,0:T(8,128)(2,1)} %param.6) | copy-start | bytes 1572868
  8.0 155.0 %all-gather.3.cloned.1.call-start = ((), (), s32[]{:S(2)}) async-start(), calls=%async_computation.9 | async-start | bytes 10485760 | tf_op jit(solution)/shard_map/all_gather | solution.py:81
  11.7 33.6 %copy-start.7 = (bf16[1,128,2048]{2,1,0:T(8,128)(2,1)S(1)}, bf16[1,128,2048]{2,1,0:T(8,128)(2,1)}, u32[]{:S(2)}) copy-start(bf16[1,128,2048]{2,1,0:T(8,128)(2,1)} %param.7) | copy-start | bytes 1572868
  24.2 17.4 %all-to-all-start = ((bf16[2,2,65536]{2,1,0:T(2,128)(2,1)}), bf16[2,2,65536]{2,1,0:T(2,128)(2,1)S(1)}, u32[]{:S(2)}, u32[]{:S(2)}) async-start(bf16[2,2,65536]{2,1,0:T(2,128)(2,1)} %reshape.80), calls=%async_computation | async-start | bytes 1048576 | tf_op jit(solution)/shard_map/all_to_all | solution.py:85
  41.6 16.9 %all-to-all-start.1 = ((bf16[2,2,65536]{2,1,0:T(2,128)(2,1)}), bf16[2,2,65536]{2,1,0:T(2,128)(2,1)S(1)}, u32[]{:S(2)}, u32[]{:S(2)}) async-start(bf16[2,2,65536]{2,1,0:T(2,128)(2,1)} %reshape.82), calls=%async_computation.1 | async-start | bytes 1048576 | tf_op jit(solution)/shard_map/all_to_all | solution.py:86
  58.5 12.2 %all-to-all-start.3 = ((bf16[2,2,65536]{2,1,0:T(2,128)(2,1)}), bf16[2,2,65536]{2,1,0:T(2,128)(2,1)S(1)}, u32[]{:S(2)}, u32[]{:S(2)}) async-start(bf16[2,2,65536]{2,1,0:T(2,128)(2,1)} %reshape.78), calls=%async_computation.3 | async-start | bytes 1048576 | tf_op jit(solution)/shard_map/all_to_all | solution.py:87
  62.0 370.5 %reduce-scatter.2.cloned.1.call-start = ((), (), s32[]{:S(2)}) async-start(), calls=%async_computation.10 | async-start | bytes 18874368 | tf_op jit(solution)/shard_map/reduce_scatter | solution.py:97
  71.5 11.1 %copy-start.13 = (bf16[1,2,128,1024]{3,2,1,0:T(8,128)(2,1)}, bf16[1,2,128,1024]{3,2,1,0:T(8,128)(2,1)S(1)}, u32[]{:S(2)}) copy-start(bf16[1,2,128,1024]{3,2,1,0:T(8,128)(2,1)S(1)} %copy.62) | copy-start | bytes 1572868
  81.0 1.6 copy-start.3
  82.9 0.8 copy-start.11
  172.5 34.8 %copy-start.4 = (f32[256,256]{0,1:T(8,128)S(1)}, f32[256,256]{0,1:T(8,128)}, u32[]{:S(2)}) copy-start(f32[256,256]{0,1:T(8,128)} %copy-done.3) | copy-start | bytes 786436
  207.3 1.9 copy-start.15
  208.9 16.1 %copy-start.2 = (bf16[1,2,128,1024]{3,2,1,0:T(8,128)(2,1)S(1)}, bf16[1,2,128,1024]{3,2,1,0:T(8,128)(2,1)}, u32[]{:S(2)}) copy-start(bf16[1,2,128,1024]{3,2,1,0:T(8,128)(2,1)} %copy.56) | copy-start | bytes 1572868
  209.1 0.8 copy-start.12
  216.9 8.3 %copy-start.5 = (bf16[1,2,128,1024]{3,2,1,0:T(8,128)(2,1)S(1)}, bf16[1,2,128,1024]{3,2,1,0:T(8,128)(2,1)}, u32[]{:S(2)}) copy-start(bf16[1,2,128,1024]{3,2,1,0:T(8,128)(2,1)} %copy.58) | copy-start | bytes 1572868
  219.1 260.7 %all-to-all-start.6 = ((bf16[2,2,65536]{2,1,0:T(2,128)(2,1)}), bf16[2,2,65536]{2,1,0:T(2,128)(2,1)S(1)}, u32[]{:S(2)}, u32[]{:S(2)}) async-start(bf16[2,2,65536]{2,1,0:T(2,128)(2,1)} %reshape.88), calls=%async_computation.6 | async-start | bytes 1048576 | tf_op jit(solution)/shard_map/all_to_all | solution.py:95
  222.6 248.7 %all-reduce.2.cloned.1.call-start = ((), (), s32[]{:S(2)}) async-start(), calls=%async_computation.11 | async-start | bytes 2097152 | tf_op jit(solution)/shard_map/psum | solution.py:103
  222.6 4.5 copy-start.14
  222.6 4.5 copy-start.16
  228.6 0.8 copy-start.8
  229.6 0.8 copy-start.10
  230.4 205.1 %copy-start.9 = (bf16[256,1024]{0,1:T(8,128)(2,1)S(1)}, bf16[256,1024]{0,1:T(8,128)(2,1)}, u32[]{:S(2)}) copy-start(bf16[256,1024]{0,1:T(8,128)(2,1)} %copy-done.8) | copy-start | bytes 1572868
  435.3 81.6 %all-gather.5.cloned.1.call-start = ((), (), s32[]{:S(2)}) async-start(), calls=%async_computation.12 | async-start | bytes 3145728 | tf_op jit(solution)/shard_map/all_gather | solution.py:104
  479.8 17.5 %all-to-all-start.4 = ((bf16[2,2,65536]{2,1,0:T(2,128)(2,1)}), bf16[2,2,65536]{2,1,0:T(2,128)(2,1)S(1)}, u32[]{:S(2)}, u32[]{:S(2)}) async-start(bf16[2,2,65536]{2,1,0:T(2,128)(2,1)} %reshape.84), calls=%async_computation.4 | async-start | bytes 1048576 | tf_op jit(solution)/shard_map/all_to_all | solution.py:93
  497.3 17.3 %all-to-all-start.5 = ((bf16[2,2,65536]{2,1,0:T(2,128)(2,1)}), bf16[2,2,65536]{2,1,0:T(2,128)(2,1)S(1)}, u32[]{:S(2)}, u32[]{:S(2)}) async-start(bf16[2,2,65536]{2,1,0:T(2,128)(2,1)} %reshape.86), calls=%async_computation.5 | async-start | bytes 1048576 | tf_op jit(solution)/shard_map/all_to_all | solution.py:94
  515.3 5.7 %copy-start.1 = (bf16[1,128,2048]{2,1,0:T(8,128)(2,1)S(1)}, bf16[1,128,2048]{2,1,0:T(8,128)(2,1)}, u32[]{:S(2)}) copy-start(bf16[1,128,2048]{2,1,0:T(8,128)(2,1)} %param.8) | copy-start | bytes 1572868
Sparse Core Ops, SparseCore 0:
  10.4 152.5 all-gather.2
Sparse Core Ops, SparseCore 1:
  115.1 317.4 reduce-scatter.1
  435.4 35.7 all-reduce.1
  472.7 44.1 all-gather.4
where the time goes:
time: 538 us; the launch traced here: 529 us
  waiting for transfers between devices  305 us (57%)
  other arithmetic  73.5 us (14%)
  local copies, waits for them, and re-layouts  44.6 us (8%)
  matrix products  38.3 us (7%)
  blocking collectives  28.8 us (5%)
  starting transfers between devices  22.2 us (4%)
  between operations  16.5 us (3%)
    reduce_scatter x1, waiting for transfers between devices, body(): lax.psum_scatter(jnp.einsum('btr,btd->rd', attended, cotangent, preferred...  201 us
    unnamed x8, other arithmetic  63.6 us
    all_gather x1, waiting for transfers between devices, body(): lax.all_gather(out_weight, 'fsdp', axis=0, tiled=True)  48.1 us
    psum x1, waiting for transfers between devices, body(): shares = lax.psum(shares.astype(jnp.bfloat16), 'dp').astype(jnp.float32)  34.4 us
    unnamed x65, local copies, waits for them, and re-layouts  28.2 us
    all_to_all x1, blocking collectives, body(): lax.all_to_all(grad_out, 'seq', split_axis=2, concat_axis=1, tiled=True)  17.7 us
    all_to_all x1, blocking collectives, body(): lax.all_to_all(head_results[0], 'seq', split_axis=1, concat_axis=2, tiled...  11.1 us
  transfers between devices with their start and end apart: 10, of which 7 were waited for; matrix products, arithmetic and copies ran while one was open for 28% of the time, Pallas kernels for 0%

commit v1 on v0

--- a/solution.py
+++ b/solution.py
@@ -4,6 +4,19 @@
 from jax.sharding import PartitionSpec as P
 
 DH = 128
+
+
+def gather_around(x, axis, dim):
+    ways = lax.axis_size(axis)
+    up = [(d, (d + 1) % ways) for d in range(ways)]
+    down = [(d, (d - 1) % ways) for d in range(ways)]
+    earlier, later = ([x], [x])
+    for _ in range(ways // 2):
+        earlier.append(lax.ppermute(earlier[-1], axis, up))
+    for _ in range((ways - 1) // 2):
+        later.append(lax.ppermute(later[-1], axis, down))
+    line = jnp.concatenate([*earlier[::-1], *later[1:]], axis=dim)
+    return jnp.roll(line, (lax.axis_index(axis) - ways // 2) * x.shape[dim], axis=dim)
 
 
 def head_backward(query_head, key_head, value_head, grad_head, block_rows):
@@ -78,7 +91,7 @@
     grad_out = jnp.einsum(
         "btd,rd->btr",
         cotangent,
-        lax.all_gather(out_weight, "fsdp", axis=0, tiled=True),
+        gather_around(out_weight, "fsdp", 0),
         preferred_element_type=jnp.float32,
     ).astype(jnp.bfloat16)
     query_heads, key_heads, value_heads, grad_heads = (

time: 538 us -> 636 us (1.18)
  starting transfers between devices: 22.2 us -> 64.6 us
  matrix products: 38.3 us -> 62 us
  local copies, waits for them, and re-layouts: 44.6 us -> 67 us
  waiting for transfers between devices: 305 us -> 314 us
    ppermute x0 -> x3, waiting for transfers between devices: none -> 227 us  [the longest x2 158 us: gather_around(): earlier.append(lax.ppermute(earlier[-1], axis, up))]
    reduce_scatter x1, waiting for transfers between devices: 201 us -> 42 us  [body(): lax.psum_scatter(jnp.einsum('btr,btd->rd', attended, cotangent, preferred...]
    all_gather x1 -> x0, waiting for transfers between devices: 48.1 us -> none  [body(): lax.all_gather(out_weight, 'fsdp', axis=0, tiled=True)]
    ppermute x0 -> x3, starting transfers between devices: none -> 41.8 us  [the longest x1 22.8 us: gather_around(): later.append(lax.ppermute(later[-1], axis, down))]
    unnamed x65 -> x108, local copies, waits for them, and re-layouts: 28.2 us -> 41.1 us
    dot_general x8, matrix products: 3.64 us -> 13.1 us  [visit(): jnp.einsum('qk,qd->kd', grad_scores, query_block, preferred_element_type=...]
    dot_general x8, matrix products: 1.83 us -> 10.8 us  [visit(): jnp.einsum('qk,qd->kd', weights_half, grad_block, preferred_element_type=...]
    dot_general x8, matrix products: 1.74 us -> 8.82 us  [visit(): jnp.einsum('qk,kd->qd', grad_scores, key_head, preferred_element_type=jnp...]
  transfers between devices with their start and end apart: 10 -> 12, of which waited for: 7 -> 8; matrix products, arithmetic and copies ran while one was open for 28% -> 24% of each run, Pallas kernels for 0% -> 0%
where the time goes in v1:
time: 636 us; the launch traced here: 625 us
  waiting for transfers between devices  314 us (49%)
  other arithmetic  77.5 us (12%)
  local copies, waits for them, and re-layouts  67 us (11%)
  starting transfers between devices  64.6 us (10%)
  matrix products  62 us (10%)
  blocking collectives  25.4 us (4%)
  between operations  15.1 us (2%)
    ppermute x2, waiting for transfers between devices, gather_around(): earlier.append(lax.ppermute(earlier[-1], axis, up))  158 us
    ppermute x1, waiting for transfers between devices, gather_around(): later.append(lax.ppermute(later[-1], axis, down))  68.7 us
    unnamed x8, other arithmetic  63 us
    reduce_scatter x1, waiting for transfers between devices, body(): lax.psum_scatter(jnp.einsum('btr,btd->rd', attended, cotangent, preferred...  42 us
    unnamed x108, local copies, waits for them, and re-layouts  41.1 us
    psum x1, waiting for transfers between devices, body(): shares = lax.psum(shares.astype(jnp.bfloat16), 'dp').astype(jnp.float32)  31.3 us
    ppermute x1, starting transfers between devices, gather_around(): later.append(lax.ppermute(later[-1], axis, down))  22.8 us
    ppermute x2, starting transfers between devices, gather_around(): earlier.append(lax.ppermute(earlier[-1], axis, up))  19 us
  transfers between devices with their start and end apart: 12, of which 8 were waited for; matrix products, arithmetic and copies ran while one was open for 24% of the time, Pallas kernels for 0%

profile of v1, /device:TPU:0, one launch (start us, length us, event | category | flops | bytes accessed | tf_op | source)
XLA Modules:
  0.0 625.4 jit_solution(1327228646953020909)
XLA Ops:
  10.1 11.5 %reduce = bf16[2048,128]{1,0:T(8,128)(2,1)S(1)} reduce(bf16[2048,1,128]{2,1,0:T(2,128)(2,1)S(1)} %bitcast.296, bf16[]{:T(256)} %broadcast.91), dimensions={1}, to_apply=%bitcast.179.reduce_sub_computation | reduce | bytes 1048578
  22.5 4.2 all-to-all-start.1
  29.1 11.5 %reduce.1 = bf16[2048,128]{1,0:T(8,128)(2,1)S(1)} reduce(bf16[2048,1,128]{2,1,0:T(2,128)(2,1)S(1)} %bitcast.302, bf16[]{:T(256)} %broadcast.91), dimensions={1}, to_apply=%bitcast.177.reduce_sub_computation | reduce | bytes 1048578
  41.4 3.7 all-to-all-start
  47.6 11.5 %reduce.2 = bf16[2048,128]{1,0:T(8,128)(2,1)S(1)} reduce(bf16[2048,1,128]{2,1,0:T(2,128)(2,1)S(1)} %bitcast.303, bf16[]{:T(256)} %broadcast.91), dimensions={1}, to_apply=%bitcast.175.reduce_sub_computation | reduce | bytes 1048578
  60.7 4.2 all-to-all-start.3
  69.7 4.1 all-to-all-done.3
  88.9 4.5 reduce.7
  94.8 10.8 %all_to_all.141 = bf16[2,2,65536]{2,1,0:T(2,128)(2,1)} all-to-all(bf16[2,2,65536]{2,1,0:T(2,128)(2,1)S(1)} %reshape.90), channel_id=1, replica_groups=mesh['dp'=4,'fsdp'=4,'seq'=2] {'seq'}, dimensions={0} | all-to-all | bytes 1048576 | tf_op jit(solution)/shard_map/all_to_all | solution.py:105
  110.1 9.2 %fusion.56 = f32[2048,2048]{1,0:T(8,128)} fusion(bf16[128,2048]{0,1:T(8,128)(2,1)} %bitcast.304, bf16[1,128,2048]{2,1,0:T(8,128)(2,1)S(1)} %copy-done), kind=kOutput, calls=%fused_computation.93 | convolution fusion | flops 1073741824 | bytes 17825792 | tf_op jit(solution)/shard_map/btr,btd->rd/dot_general | solution.py:111
  120.9 85.3 %collective-permute-done = bf16[512,2048]{1,0:T(8,128)(2,1)} collective-permute-done((bf16[512,2048]{1,0:T(8,128)(2,1)S(1)}, bf16[512,2048]{1,0:T(8,128)(2,1)}, u32[]{:S(2)}, u32[]{:S(2)}) %collective-permute-start) | collective-permute-done | bytes 2097184 | tf_op jit(solution)/shard_map/ppermute | solution.py:15
  206.2 17.5 %collective-permute-start.1 = (bf16[512,2048]{1,0:T(8,128)(2,1)}, bf16[512,2048]{1,0:T(8,128)(2,1)}, u32[]{:S(2)}, u32[]{:S(2)}) collective-permute-start(bf16[512,2048]{1,0:T(8,128)(2,1)} %collective-permute-done), channel_id=1, source_target_pairs={{0,2},{2,4},{4,6},{6,0},{1,3},{3,5},{5,7},{7,1},{8,10},{10,12},{12... | collective-permute-start | bytes 6291464 | tf_op jit(solution)/shard_map/ppermute | solution.py:15
  223.7 22.8 %collective-permute-start.2 = (bf16[512,2048]{1,0:T(8,128)(2,1)S(1)}, bf16[512,2048]{1,0:T(8,128)(2,1)}, u32[]{:S(2)}, u32[]{:S(2)}) collective-permute-start(bf16[512,2048]{1,0:T(8,128)(2,1)S(1)} %copy-done.1), channel_id=1, source_target_pairs={{0,6},{2,0},{4,2},{6,4},{1,7},{3,1},{5,3},{7,5},{8,14},{10,8},{12,... | collective-permute-start | bytes 6291464 | tf_op jit(solution)/shard_map/ppermute | solution.py:17
  246.5 73.0 %collective-permute-done.1 = bf16[512,2048]{1,0:T(8,128)(2,1)} collective-permute-done((bf16[512,2048]{1,0:T(8,128)(2,1)}, bf16[512,2048]{1,0:T(8,128)(2,1)}, u32[]{:S(2)}, u32[]{:S(2)}) %collective-permute-start.1) | collective-permute-done | bytes 2097184 | tf_op jit(solution)/shard_map/ppermute | solution.py:15
  323.2 68.7 %collective-permute-done.2 = bf16[512,2048]{1,0:T(8,128)(2,1)} collective-permute-done((bf16[512,2048]{1,0:T(8,128)(2,1)S(1)}, bf16[512,2048]{1,0:T(8,128)(2,1)}, u32[]{:S(2)}, u32[]{:S(2)}) %collective-permute-start.2) | collective-permute-done | bytes 2097184 | tf_op jit(solution)/shard_map/ppermute | solution.py:17
  401.8 8.1 %copy.83 = bf16[1,128,2048]{1,0,2:T(2,128)(2,1)S(1)} copy(bf16[1,128,2048]{1,2,0:T(8,128)(2,1)S(1)} %fusion.5) | data formatting | bytes 1048576 | tf_op jit(solution)/shard_map/convert_element_type | solution.py:96
  409.9 12.3 %reduce.3 = bf16[2048,128]{1,0:T(8,128)(2,1)} reduce(bf16[2048,1,128]{2,1,0:T(2,128)(2,1)S(1)} %bitcast.299, bf16[]{:T(256)} %broadcast.91), dimensions={1}, to_apply=%bitcast.271.reduce_sub_computation | reduce | bytes 1048578
  423.3 14.6 %all_to_all.142 = bf16[2,2,65536]{2,1,0:T(2,128)(2,1)} all-to-all(bf16[2,2,65536]{2,1,0:T(2,128)(2,1)S(1)} %reshape.76), channel_id=1, replica_groups=mesh['dp'=4,'fsdp'=4,'seq'=2] {'seq'}, dimensions={0} | all-to-all | bytes 1048576 | tf_op jit(solution)/shard_map/all_to_all | solution.py:101
  464.6 2.5 copy.63
  467.1 4.5 reduce.4
  473.6 3.5 all-to-all-start.4
  486.0 42.0 %reduce-scatter.2.cloned.1.call-done = f32[256,2048]{1,0:T(8,128)} async-done(((f32[2048,2048]{1,0:T(8,128)}), f32[256,2048]{1,0:T(8,128)}) %reduce-scatter.2.cloned.1.call-update) | async-done | bytes 2097168 | tf_op jit(solution)/shard_map/reduce_scatter | solution.py:110
  528.0 2.7 convert_element_type.244
  534.9 31.3 %all-reduce.2.cloned.1.call-done = bf16[256,2048]{1,0:T(8,128)(2,1)} async-done(((bf16[256,2048]{1,0:T(8,128)(2,1)}), bf16[256,2048]{1,0:T(8,128)(2,1)}) %all-reduce.2.cloned.1.call-update) | async-done | bytes 1048592 | tf_op jit(solution)/shard_map/psum | solution.py:116
  572.2 2.7 copy.65
  574.9 3.7 reduce.5
  581.4 3.5 all-to-all-start.5
  590.8 3.7 reduce.6
  595.6 3.8 all-to-all-done.5
  599.4 3.5 all-to-all-start.6
  606.8 5.4 all-to-all-done.6
  614.2 4.2 convert_multiply_fusion
  (195 shorter events, 115.7 us)
Async XLA Ops:
  7.2 102.9 %copy-start = (bf16[1,128,2048]{2,1,0:T(8,128)(2,1)S(1)}, bf16[1,128,2048]{2,1,0:T(8,128)(2,1)}, u32[]{:S(2)}) copy-start(bf16[1,128,2048]{2,1,0:T(8,128)(2,1)} %param.8) | copy-start | bytes 1572868
  22.5 18.9 %all-to-all-start.1 = ((bf16[2,2,65536]{2,1,0:T(2,128)(2,1)}), bf16[2,2,65536]{2,1,0:T(2,128)(2,1)S(1)}, u32[]{:S(2)}, u32[]{:S(2)}) async-start(bf16[2,2,65536]{2,1,0:T(2,128)(2,1)} %reshape.82), calls=%async_computation.1 | async-start | bytes 1048576 | tf_op jit(solution)/shard_map/all_to_all | solution.py:99
  41.4 19.3 %all-to-all-start = ((bf16[2,2,65536]{2,1,0:T(2,128)(2,1)}), bf16[2,2,65536]{2,1,0:T(2,128)(2,1)S(1)}, u32[]{:S(2)}, u32[]{:S(2)}) async-start(bf16[2,2,65536]{2,1,0:T(2,128)(2,1)} %reshape.80), calls=%async_computation | async-start | bytes 1048576 | tf_op jit(solution)/shard_map/all_to_all | solution.py:98
  60.7 13.1 %all-to-all-start.3 = ((bf16[2,2,65536]{2,1,0:T(2,128)(2,1)}), bf16[2,2,65536]{2,1,0:T(2,128)(2,1)}, u32[]{:S(2)}, u32[]{:S(2)}) async-start(bf16[2,2,65536]{2,1,0:T(2,128)(2,1)} %reshape.78), calls=%async_computation.3 | async-start | bytes 1048576 | tf_op jit(solution)/shard_map/all_to_all | solution.py:100
  65.0 463.0 %reduce-scatter.2.cloned.1.call-start = ((), (), s32[]{:S(2)}) async-start(), calls=%async_computation.9 | async-start | bytes 18874368 | tf_op jit(solution)/shard_map/reduce_scatter | solution.py:110
  66.7 376.1 %copy-start.26 = (f32[256]{0:T(256)}, f32[256]{0:T(256)S(1)}, u32[]{:S(2)}) copy-start(f32[256]{0:T(256)S(1)} %get-tuple-element.152) | copy-start | bytes 3076
  67.6 378.6 %copy-start.25 = (f32[256]{0:T(256)}, f32[256]{0:T(256)S(1)}, u32[]{:S(2)}) copy-start(f32[256]{0:T(256)S(1)} %get-tuple-element.165) | copy-start | bytes 3076
  68.5 381.1 %copy-start.24 = (f32[256]{0:T(256)}, f32[256]{0:T(256)S(1)}, u32[]{:S(2)}) copy-start(f32[256]{0:T(256)S(1)} %get-tuple-element.169) | copy-start | bytes 3076
  68.8 41.3 %copy-start.8 = (f32[256,256]{0,1:T(8,128)}, f32[256,256]{0,1:T(8,128)S(1)}, u32[]{:S(2)}) copy-start(f32[256,256]{0,1:T(8,128)S(1)} %get-tuple-element.183) | copy-start | bytes 786436
  68.8 384.1 %copy-start.23 = (f32[256]{0:T(256)}, f32[256]{0:T(256)S(1)}, u32[]{:S(2)}) copy-start(f32[256]{0:T(256)S(1)} %get-tuple-element.182) | copy-start | bytes 3076
  69.0 41.0 %copy-start.6 = (f32[256,256]{0,1:T(8,128)}, f32[256,256]{0,1:T(8,128)S(1)}, u32[]{:S(2)}) copy-start(f32[256,256]{0,1:T(8,128)S(1)} %get-tuple-element.187) | copy-start | bytes 786436
  69.2 40.8 %copy-start.4 = (f32[256,256]{0,1:T(8,128)}, f32[256,256]{0,1:T(8,128)S(1)}, u32[]{:S(2)}) copy-start(f32[256,256]{0,1:T(8,128)S(1)} %get-tuple-element.200) | copy-start | bytes 786436
  78.6 364.3 %copy-start.34 = (f32[256]{0:T(256)}, f32[256]{0:T(256)S(1)}, u32[]{:S(2)}) copy-start(f32[256]{0:T(256)S(1)} %fusion.60) | copy-start | bytes 3076
  79.6 366.6 %copy-start.33 = (f32[256]{0:T(256)}, f32[256]{0:T(256)S(1)}, u32[]{:S(2)}) copy-start(f32[256]{0:T(256)S(1)} %fusion.62) | copy-start | bytes 3076
  80.6 369.0 %copy-start.32 = (f32[256]{0:T(256)}, f32[256]{0:T(256)S(1)}, u32[]{:S(2)}) copy-start(f32[256]{0:T(256)S(1)} %fusion.64) | copy-start | bytes 3076
  80.7 372.2 %copy-start.31 = (f32[256]{0:T(256)}, f32[256]{0:T(256)S(1)}, u32[]{:S(2)}) copy-start(f32[256]{0:T(256)S(1)} %fusion.66) | copy-start | bytes 3076
  80.8 374.4 %copy-start.30 = (f32[256]{0:T(256)}, f32[256]{0:T(256)S(1)}, u32[]{:S(2)}) copy-start(f32[256]{0:T(256)S(1)} %fusion.68) | copy-start | bytes 3076
  80.9 376.6 %copy-start.29 = (f32[256]{0:T(256)}, f32[256]{0:T(256)S(1)}, u32[]{:S(2)}) copy-start(f32[256]{0:T(256)S(1)} %fusion.70) | copy-start | bytes 3076
  80.9 378.8 %copy-start.28 = (f32[256]{0:T(256)}, f32[256]{0:T(256)S(1)}, u32[]{:S(2)}) copy-start(f32[256]{0:T(256)S(1)} %fusion.72) | copy-start | bytes 3076
  81.0 380.0 %copy-start.27 = (f32[256]{0:T(256)}, f32[256]{0:T(256)S(1)}, u32[]{:S(2)}) copy-start(f32[256]{0:T(256)S(1)} %fusion.74) | copy-start | bytes 3076
  119.3 86.9 %collective-permute-start = (bf16[512,2048]{1,0:T(8,128)(2,1)S(1)}, bf16[512,2048]{1,0:T(8,128)(2,1)}, u32[]{:S(2)}, u32[]{:S(2)}) collective-permute-start(bf16[512,2048]{1,0:T(8,128)(2,1)S(1)} %copy-done.1), channel_id=1, source_target_pairs={{0,2},{2,4},{4,6},{6,0},{1,3},{3,5},{5,7},{7,1},{8,10},{10,12},{12... | collective-permute-start | bytes 6291464 | tf_op jit(solution)/shard_map/ppermute | solution.py:15
  206.2 113.2 %collective-permute-start.1 = (bf16[512,2048]{1,0:T(8,128)(2,1)}, bf16[512,2048]{1,0:T(8,128)(2,1)}, u32[]{:S(2)}, u32[]{:S(2)}) collective-permute-start(bf16[512,2048]{1,0:T(8,128)(2,1)} %collective-permute-done), channel_id=1, source_target_pairs={{0,2},{2,4},{4,6},{6,0},{1,3},{3,5},{5,7},{7,1},{8,10},{10,12},{12... | collective-permute-start | bytes 6291464 | tf_op jit(solution)/shard_map/ppermute | solution.py:15
  223.7 168.2 %collective-permute-start.2 = (bf16[512,2048]{1,0:T(8,128)(2,1)S(1)}, bf16[512,2048]{1,0:T(8,128)(2,1)}, u32[]{:S(2)}, u32[]{:S(2)}) collective-permute-start(bf16[512,2048]{1,0:T(8,128)(2,1)S(1)} %copy-done.1), channel_id=1, source_target_pairs={{0,6},{2,0},{4,2},{6,4},{1,7},{3,1},{5,3},{7,5},{8,14},{10,8},{12,... | collective-permute-start | bytes 6291464 | tf_op jit(solution)/shard_map/ppermute | solution.py:17
  397.4 54.4 %copy-start.9 = (f32[256,256]{0,1:T(8,128)S(1)}, f32[256,256]{0,1:T(8,128)}, u32[]{:S(2)}) copy-start(f32[256,256]{0,1:T(8,128)} %copy-done.8) | copy-start | bytes 786436
  397.4 56.7 %copy-start.7 = (f32[256,256]{0,1:T(8,128)S(1)}, f32[256,256]{0,1:T(8,128)}, u32[]{:S(2)}) copy-start(f32[256,256]{0,1:T(8,128)} %copy-done.6) | copy-start | bytes 786436
  399.3 57.1 %copy-start.5 = (f32[256,256]{0,1:T(8,128)S(1)}, f32[256,256]{0,1:T(8,128)}, u32[]{:S(2)}) copy-start(f32[256,256]{0,1:T(8,128)} %copy-done.4) | copy-start | bytes 786436
  399.3 59.4 %copy-start.3 = (f32[256,256]{0,1:T(8,128)S(1)}, f32[256,256]{0,1:T(8,128)}, u32[]{:S(2)}) copy-start(f32[256,256]{0,1:T(8,128)} %copy-done.2) | copy-start | bytes 786436
  473.6 107.8 %all-to-all-start.4 = ((bf16[2,2,65536]{2,1,0:T(2,128)(2,1)}), bf16[2,2,65536]{2,1,0:T(2,128)(2,1)S(1)}, u32[]{:S(2)}, u32[]{:S(2)}) async-start(bf16[2,2,65536]{2,1,0:T(2,128)(2,1)} %reshape.84), calls=%async_computation.4 | async-start | bytes 1048576 | tf_op jit(solution)/shard_map/all_to_all | solution.py:106
  477.1 89.1 %all-reduce.2.cloned.1.call-start = ((), (), s32[]{:S(2)}) async-start(), calls=%async_computation.10 | async-start | bytes 2097152 | tf_op jit(solution)/shard_map/psum | solution.py:116
  530.7 83.5 %all-gather.2.cloned.1.call-start = ((), (), s32[]{:S(2)}) async-start(), calls=%async_computation.11 | async-start | bytes 3145728 | tf_op jit(solution)/shard_map/all_gather | solution.py:117
  581.4 18.0 %all-to-all-start.5 = ((bf16[2,2,65536]{2,1,0:T(2,128)(2,1)}), bf16[2,2,65536]{2,1,0:T(2,128)(2,1)S(1)}, u32[]{:S(2)}, u32[]{:S(2)}) async-start(bf16[2,2,65536]{2,1,0:T(2,128)(2,1)} %reshape.86), calls=%async_computation.5 | async-start | bytes 1048576 | tf_op jit(solution)/shard_map/all_to_all | solution.py:107
  599.4 12.9 %all-to-all-start.6 = ((bf16[2,2,65536]{2,1,0:T(2,128)(2,1)}), bf16[2,2,65536]{2,1,0:T(2,128)(2,1)S(1)}, u32[]{:S(2)}, u32[]{:S(2)}) async-start(bf16[2,2,65536]{2,1,0:T(2,128)(2,1)} %reshape.88), calls=%async_computation.6 | async-start | bytes 1048576 | tf_op jit(solution)/shard_map/all_to_all | solution.py:108
  (15 other events, 143.1 us)
Sparse Core Ops, SparseCore 0:
  119.4 408.4 reduce-scatter.1
  531.0 35.1 all-reduce.1
  567.8 40.7 all-gather.1
